TPU v7x, 32 devices: a whole 2x2x4 slice. The times are simulated.
32 devices in a mesh: groups: 2 (over x), band: 16 (over z, y, core).
Axes of the slice: x: 2, y: 2, z: 4, core: 2. Of those that a mesh axis runs over, the one named last changes fastest.
Arguments:
- grid_state: bfloat16 [8192, 474], P(('groups', 'band')), parts along dimension 0, may hold values from -6 to 6
- mesh_static: float32 [3, 4096], P(None, 'band'), may hold values from -6 to 6
- encoder_senders: int32 [16, 3, 1, 128], P('band'), may hold values from 0 to 255
- encoder_receivers: int32 [16, 3, 1, 128], P('band'), may hold values from 0 to 255
- encoder_counts: int32 [16, 3], P('band'), may hold values from 0 to 128, as said below
- mesh_senders: int32 [256, 128], P('band'), may hold values from 0 to 511
- mesh_receivers: int32 [256, 128], P('band'), may hold values from 0 to 255
- halo_rows: int32 [16, 128], P('band'), may hold values from 0 to 255
- backward_icosa_emitters: int32 [16, 3, 2, 128], P('band'), may hold values from 0 to 255
- backward_cell_destination: int32 [16, 3, 2, 128], P('band'), may hold values from 0 to 255
- backward_active_slot_amounts: int32 [16, 3], P('band'), may hold values from 0 to 256, as said below
- grid_embed: bfloat16 [474, 512], replicated, may hold values from -0.25 to 0.25
- mesh_embed: float32 [3, 512], replicated, may hold values from -3.5 to 3.5
- encoder_source: bfloat16 [512, 512], replicated, may hold values from -0.25 to 0.25
- encoder_target: bfloat16 [512, 512], replicated, may hold values from -0.25 to 0.25
- encoder_message: bfloat16 [512, 512], replicated, may hold values from -0.25 to 0.25
- encoder_retain: bfloat16 [512, 512], replicated, may hold values from -0.25 to 0.25
- encoder_absorb: bfloat16 [512, 512], replicated, may hold values from -0.25 to 0.25
- encoder_finish: bfloat16 [512, 512], replicated, may hold values from -0.25 to 0.25
- process_source: bfloat16 [2, 512, 512], replicated, may hold values from -0.25 to 0.25
- process_target: bfloat16 [2, 512, 512], replicated, may hold values from -0.25 to 0.25
- process_retain: bfloat16 [2, 512, 512], replicated, may hold values from -0.25 to 0.25
- process_absorb: bfloat16 [2, 512, 512], replicated, may hold values from -0.25 to 0.25
- process_finish: bfloat16 [2, 512, 512], replicated, may hold values from -0.25 to 0.25
- decoder_source: bfloat16 [512, 512], replicated, may hold values from -0.25 to 0.25
- decoder_target: bfloat16 [512, 512], replicated, may hold values from -0.25 to 0.25
- decoder_message: bfloat16 [512, 512], replicated, may hold values from -0.25 to 0.25
- decoder_retain: bfloat16 [512, 512], replicated, may hold values from -0.25 to 0.25
- decoder_absorb: bfloat16 [512, 512], replicated, may hold values from -0.25 to 0.25
- readout_matrix: bfloat16 [512, 227], replicated, may hold values from -0.25 to 0.25
Outputs:
- estimated_variables: bfloat16 [8192, 227], P(('groups', 'band')), parts along dimension 0
There are 2 independent parts, one for each index of `groups`. A program takes and returns all parts, laid end to end along the dimension named above; an argument that names none is the same for every part. Nothing has to cross between parts.
Inputs may be any that keep to these rules, and one draw needn't show every extreme that they name: `encoder_counts`: the first count slots of the pair's blocks, in order, are edges; the rest are unused. Pairs with a band or patch outside 0 to 15 have count 0. `backward_active_slot_amounts`: the first count slots of the pair's blocks, in order, are edges; the rest are unused. Pairs with a band or patch outside 0 to 15 have count 0.
All inputs are finite; a program needn't handle non-finite values.
Results may differ from a plain program's by a relative error of at most 0.015.
Values may be sent and summed in bfloat16 or wider, within the bound.
A program may use at most 64 MiB of HBM per device.

v0:
```python
import jax
import jax.numpy as jnp
from jax import lax
from jax.sharding import PartitionSpec as P


def with_halo(block, sides, width):
    for axis, dim in sides:
        count = lax.axis_size(axis)
        forward = [(i, i + 1) for i in range(count - 1)]
        backward = [(target, source) for source, target in forward]
        low = lax.ppermute(
            lax.slice_in_dim(block, block.shape[dim] - width, None, axis=dim), axis, forward
        )
        high = lax.ppermute(lax.slice_in_dim(block, 0, width, axis=dim), axis, backward)
        block = jnp.concatenate([low, block, high], axis=dim)
    return block


def product(left, right):
    return jnp.dot(left, right, preferred_element_type=jnp.float32)


def norm_rows(values):
    centre = values - jnp.mean(values, axis=-1, keepdims=True)
    spread = jnp.mean(centre * centre, axis=-1, keepdims=True)
    return centre * lax.rsqrt(spread + 1e-05)


def onehot_sum(message, flat_in, node_count):
    selector = (jnp.arange(node_count, dtype=jnp.int32)[:, None] == flat_in[None, :]).astype(
        jnp.float32
    )
    return jnp.dot(
        selector, message, precision=lax.Precision.HIGHEST, preferred_element_type=jnp.float32
    )


def edge_messages(rows, receivers, counts, target, weight, node_count):
    width = rows.shape[1]
    flat_in = receivers.reshape(-1)
    joined = rows.reshape(-1, rows.shape[-1]).astype(jnp.float32) + jnp.take(
        target, flat_in, axis=0
    )
    hidden = jax.nn.silu(joined).astype(jnp.bfloat16)
    message = product(hidden, weight)
    live_slots = jnp.arange(width, dtype=jnp.int32)[None, :] < counts[:, None]
    message = jnp.where(live_slots.reshape(-1, 1), message, 0.0)
    return onehot_sum(message, flat_in, node_count).astype(jnp.bfloat16)


def mesh_sum(table, senders, receivers, target, node_count):
    flat_in = receivers.reshape(-1)
    joined = jnp.take(table, senders.reshape(-1), axis=0).astype(jnp.float32) + jnp.take(
        target, flat_in, axis=0
    )
    return onehot_sum(jax.nn.silu(joined), flat_in, node_count).astype(jnp.bfloat16)


def vertex_refresh(state, coarse_vertex_values, gathered, w_self, w_incoming, w_finish):
    inner_rows = jax.nn.silu(
        product(coarse_vertex_values, w_self) + product(gathered, w_incoming)
    ).astype(jnp.bfloat16)
    return state + norm_rows(product(inner_rows, w_finish))


def body(
    grid_state,
    mesh_static,
    encoder_senders,
    encoder_receivers,
    encoder_counts,
    mesh_senders,
    mesh_receivers,
    halo_rows,
    backward_icosa_emitters,
    backward_cell_destination,
    backward_active_slot_amounts,
    grid_embed,
    mesh_embed,
    encoder_source,
    encoder_target,
    encoder_message,
    encoder_retain,
    encoder_absorb,
    encoder_finish,
    process_source,
    process_target,
    process_retain,
    process_absorb,
    process_finish,
    decoder_source,
    decoder_target,
    decoder_message,
    decoder_retain,
    decoder_absorb,
    readout_matrix,
):
    grid_nodes = grid_state.shape[0]
    mesh_nodes = mesh_static.shape[1]
    cell_hidden_state = norm_rows(jax.nn.silu(product(grid_state, grid_embed))).astype(jnp.bfloat16)
    grid_source = product(cell_hidden_state, encoder_source).astype(jnp.bfloat16)
    enc_lists = encoder_senders[0].reshape(3, -1)
    enc_width = enc_lists.shape[1]
    leaving = jnp.concatenate(
        [jnp.take(grid_source, enc_lists[0], axis=0), jnp.take(grid_source, enc_lists[2], axis=0)],
        axis=0,
    )
    beside_all = with_halo(leaving, (("band", 0),), enc_width)
    own_rows = jnp.take(grid_source, enc_lists[1], axis=0)
    enc_rows = jnp.stack([beside_all[:enc_width], own_rows, beside_all[3 * enc_width :]], axis=0)
    mesh_state = jax.nn.silu(jnp.dot(mesh_static.T, mesh_embed, precision=lax.Precision.HIGHEST))
    mesh_low = mesh_state.astype(jnp.bfloat16)
    mesh_target = product(mesh_low, encoder_target)
    gathered = edge_messages(
        enc_rows,
        encoder_receivers[0].reshape(3, -1),
        encoder_counts[0],
        mesh_target,
        encoder_message,
        mesh_nodes,
    )
    mesh_state = vertex_refresh(
        mesh_state, mesh_low, gathered, encoder_retain, encoder_absorb, encoder_finish
    )
    rim_width = halo_rows.shape[1]
    for layer_index in range(process_source.shape[0]):
        mesh_low = mesh_state.astype(jnp.bfloat16)
        source_rows = product(mesh_low, process_source[layer_index]).astype(jnp.bfloat16)
        target_rows = product(mesh_low, process_target[layer_index])
        rim_rows = jnp.take(source_rows, halo_rows[0], axis=0)
        rims = with_halo(rim_rows, (("band", 0),), rim_width)
        extended = jnp.concatenate([rims[:rim_width], source_rows, rims[2 * rim_width :]], axis=0)
        gathered = mesh_sum(extended, mesh_senders, mesh_receivers, target_rows, mesh_nodes)
        mesh_state = vertex_refresh(
            mesh_state,
            mesh_low,
            gathered,
            process_retain[layer_index],
            process_absorb[layer_index],
            process_finish[layer_index],
        )
    mesh_low = mesh_state.astype(jnp.bfloat16)
    mesh_source = product(mesh_low, decoder_source).astype(jnp.bfloat16)
    cell_destination_state = product(cell_hidden_state, decoder_target)
    dec_lists = backward_icosa_emitters[0].reshape(3, -1)
    dec_width = dec_lists.shape[1]
    table = with_halo(mesh_source, (("band", 0),), mesh_nodes)
    shifted = dec_lists + jnp.arange(3, dtype=jnp.int32)[:, None] * mesh_nodes
    inbound_messages = jnp.take(table, shifted.reshape(-1), axis=0).reshape(3, dec_width, -1)
    summed = edge_messages(
        inbound_messages,
        backward_cell_destination[0].reshape(3, -1),
        backward_active_slot_amounts[0],
        cell_destination_state,
        decoder_message,
        grid_nodes,
    )
    inner_rows = jax.nn.silu(
        product(cell_hidden_state, decoder_retain) + product(summed, decoder_absorb)
    ).astype(jnp.bfloat16)
    return product(inner_rows, readout_matrix).astype(jnp.bfloat16)


def solution(mesh):
    placed = (
        P(("groups", "band"), None),
        P(None, "band"),
        P("band", None, None, None),
        P("band", None, None, None),
        P("band", None),
        P("band", None),
        P("band", None),
        P("band", None),
        P("band", None, None, None),
        P("band", None, None, None),
        P("band", None),
        P(),
        P(),
        P(),
        P(),
        P(),
        P(),
        P(),
        P(),
        P(),
        P(),
        P(),
        P(),
        P(),
        P(),
        P(),
        P(),
        P(),
        P(),
        P(),
    )
    return jax.shard_map(
        body, mesh=mesh, in_specs=placed, out_specs=P(("groups", "band"), None), check_vma=False
    )
```

profile of v0, /device:TPU:13, one launch (start us, length us, event | category | flops | bytes accessed | tf_op | source)
XLA Modules:
  0.0 129.0 jit_solution(2858005939269703067)
XLA Ops:
  0.0 1.7 %fusion.123 = (f32[256]{0:T(256)S(1)}, f32[256,512]{1,0:T(8,128)S(1)}) fusion(bf16[256,474]{0,1:T(8,128)(2,1)} %param.36, bf16[474,512]{1,0:T(8,128)(2,1)} %param.47), kind=kOutput, calls=%fused_computation.201 | convolution fusion | flops 124911360 | bytes 1253376 | tf_op jit(solution)/shard_map/dot_general | solution.py:21
  3.6 3.7 %collective-permute-start = (bf16[128,512]{1,0:T(8,128)(2,1)S(1)}, bf16[128,512]{1,0:T(8,128)(2,1)}, u32[]{:S(2)}, u32[]{:S(2)}) collective-permute-start(bf16[128,512]{1,0:T(8,128)(2,1)S(1)} %broadcast_select_fusion.3), channel_id=1, source_target_pairs={{0,1},{1,2},{2,3},{3,4},{4,5},{5,6},{6,7},{7,8},{8,9},{9,10},{10,1... | collective-permute-start | bytes 393224 | tf_op jit(solution)/shard_map/ppermute | solution.py:12
  8.3 2.1 %collective-permute-start.1 = (bf16[128,512]{1,0:T(8,128)(2,1)S(1)}, bf16[128,512]{1,0:T(8,128)(2,1)}, u32[]{:S(2)}, u32[]{:S(2)}) collective-permute-start(bf16[128,512]{1,0:T(8,128)(2,1)S(1)} %broadcast_select_fusion.2), channel_id=1, source_target_pairs={{1,0},{2,1},{3,2},{4,3},{5,4},{6,5},{7,6},{8,7},{9,8},{10,9},{11,1... | collective-permute-start | bytes 393224 | tf_op jit(solution)/shard_map/ppermute | solution.py:15
  19.4 1.8 %gather_fusion = f32[384,512]{1,0:T(8,128)S(1)} fusion(f32[256,512]{1,0:T(8,128)S(1)} %fusion.91, s32[1024]{0:T(1024)} %pad_clamp_fusion.3), kind=kCustom, calls=%fused_computation.9 | custom fusion | bytes 1574400 | tf_op jit(solution)/shard_map/jit(_take)/gather | solution.py:42
  21.2 1.3 %fusion.98 = s32[768]{0:T(1024)} fusion(s32[768,1]{0,1:T(1,128)} %bitcast.121), kind=kLoop, calls=%fused_computation.156 | loop fusion | flops 2304 | bytes 6144 | tf_op jit(solution)/shard_map/jit(_take)/jit(_where)/select_n | solution.py:42
  23.5 1.6 %convolution_select_fusion = f32[384,512]{1,0:T(8,128)S(1)} fusion(bf16[512,512]{1,0:T(8,128)(2,1)} %param.51, bf16[384,512]{1,0:T(8,128)(2,1)S(1)} %bitcast.117, f32[384,512]{1,0:T(8,128)S(1)} %gather_fusion, pred[384]{0:T(512)(128)(4,1)} %compare_and_fusion.8, pred[384]{0:T(512)(128)(4,1)} %fusion.99), kind=kOutput, calls=%fused_computation.42 | convolution fusion | flops 203096064 | bytes 2491136 | tf_op jit(solution)/shard_map/dot_general | solution.py:21
  25.8 1.9 %fusion.124 = (f32[256]{0:T(256)S(1)}, f32[256,512]{1,0:T(8,128)S(1)}) fusion(bf16[512,512]{1,0:T(8,128)(2,1)} %param.54, f32[256,512]{1,0:T(8,128)S(1)} %copy-done.5, bf16[256,512]{1,0:T(8,128)(2,1)S(1)} %convolution_convert_fusion.4, bf16[512,512]{1,0:T(8,128)(2,1)} %param.53), kind=kOutput, calls=%fused_computation.202 | convolution fusion | flops 269352704 | bytes 2360320 | tf_op jit(solution)/shard_map/dot_general | solution.py:21
  30.3 4.5 %collective-permute-start.2 = (bf16[128,512]{1,0:T(8,128)(2,1)S(1)}, bf16[128,512]{1,0:T(8,128)(2,1)S(1)}, u32[]{:S(2)}, u32[]{:S(2)}) collective-permute-start(bf16[128,512]{1,0:T(8,128)(2,1)S(1)} %broadcast_select_fusion.1), channel_id=1, source_target_pairs={{0,1},{1,2},{2,3},{3,4},{4,5},{5,6},{6,7},{7,8},{8,9},{9,10},{10,1... | collective-permute-start | bytes 393224 | tf_op jit(solution)/shard_map/ppermute | solution.py:12
  34.9 1.9 %collective-permute-start.3 = (bf16[128,512]{1,0:T(8,128)(2,1)S(1)}, bf16[128,512]{1,0:T(8,128)(2,1)S(1)}, u32[]{:S(2)}, u32[]{:S(2)}) collective-permute-start(bf16[128,512]{1,0:T(8,128)(2,1)S(1)} %broadcast_select_fusion.1), channel_id=1, source_target_pairs={{1,0},{2,1},{3,2},{4,3},{5,4},{6,5},{7,6},{8,7},{9,8},{10,9},{11,1... | collective-permute-start | bytes 393224 | tf_op jit(solution)/shard_map/ppermute | solution.py:15
  36.8 1.3 %fusion.53 = f32[256,512]{1,0:T(8,128)S(1)} fusion(bf16[2,512,512]{2,1,0:T(8,128)(2,1)} %param.56, f32[256,512]{1,0:T(8,128)S(1)} %multiply_add_fusion.1), kind=kOutput, calls=%fused_computation.80 | convolution fusion | flops 134348800 | bytes 1572864 | tf_op jit(solution)/shard_map/dot_general | solution.py:21
  38.1 1.3 %fusion.56 = f32[256,512]{1,0:T(8,128)S(1)} fusion(bf16[2,512,512]{2,1,0:T(8,128)(2,1)} %param.57, f32[256,512]{1,0:T(8,128)S(1)} %multiply_add_fusion.1), kind=kOutput, calls=%fused_computation.83 | convolution fusion | flops 134348800 | bytes 1572864 | tf_op jit(solution)/shard_map/dot_general | solution.py:21
  39.5 8.9 %gather_fusion.8 = f32[2048,512]{1,0:T(8,128)} fusion(f32[256,512]{1,0:T(8,128)S(1)} %fusion.53, s32[2048]{0:T(1024)S(1)} %fusion.96), kind=kCustom, calls=%fused_computation.2.clone | custom fusion | bytes 8396800 | tf_op jit(solution)/shard_map/jit(_take)/gather | solution.py:54
  48.5 9.2 %gather_fusion.7 = bf16[2048,512]{1,0:T(8,128)(2,1)} fusion(bf16[512,512]{1,0:T(8,128)(2,1)S(1)} %pad_maximum_fusion.1, s32[2048]{0:T(1024)S(1)} %fusion.95), kind=kCustom, calls=%fused_computation.1.clone | custom fusion | bytes 4202496 | tf_op jit(solution)/shard_map/jit(_take)/gather | solution.py:54
  57.7 6.3 %fusion.29 = bf16[256,512]{1,0:T(8,128)(2,1)S(1)} fusion(f32[2048,512]{1,0:T(8,128)} %gather_fusion.8, bf16[2048,512]{1,0:T(8,128)(2,1)} %gather_fusion.7, pred[2048]{0:T(1024)(128)(4,1)S(1)} %copy-done.24, pred[2048]{0:T(1024)(128)(4,1)S(1)} %copy-done.26, s32[2048]{0:T(1024)S(1)} %bitcast.118), kind=kOutput, calls=%fused_computation.53 | convolution fusion | flops 3230269440 | bytes 6565888 | tf_op jit(solution)/shard_map/dot_general | solution.py:34
  64.0 1.9 %fusion.125 = (f32[256]{0:T(256)S(1)}, f32[256,512]{1,0:T(8,128)S(1)}) fusion(bf16[2,512,512]{2,1,0:T(8,128)(2,1)} %param.59, f32[256,512]{1,0:T(8,128)S(1)} %fusion.56, bf16[256,512]{1,0:T(8,128)(2,1)S(1)} %fusion.29, bf16[2,512,512]{2,1,0:T(8,128)(2,1)} %param.58), kind=kOutput, calls=%fused_computation.203 | convolution fusion | flops 269352704 | bytes 2360320 | tf_op jit(solution)/shard_map/dot_general | solution.py:21
  68.5 4.5 %collective-permute-start.4 = (bf16[128,512]{1,0:T(8,128)(2,1)S(1)}, bf16[128,512]{1,0:T(8,128)(2,1)S(1)}, u32[]{:S(2)}, u32[]{:S(2)}) collective-permute-start(bf16[128,512]{1,0:T(8,128)(2,1)S(1)} %broadcast_select_fusion), channel_id=1, source_target_pairs={{0,1},{1,2},{2,3},{3,4},{4,5},{5,6},{6,7},{7,8},{8,9},{9,10},{10,1... | collective-permute-start | bytes 393224 | tf_op jit(solution)/shard_map/ppermute | solution.py:12
  73.0 2.1 %collective-permute-start.5 = (bf16[128,512]{1,0:T(8,128)(2,1)S(1)}, bf16[128,512]{1,0:T(8,128)(2,1)S(1)}, u32[]{:S(2)}, u32[]{:S(2)}) collective-permute-start(bf16[128,512]{1,0:T(8,128)(2,1)S(1)} %broadcast_select_fusion), channel_id=1, source_target_pairs={{1,0},{2,1},{3,2},{4,3},{5,4},{6,5},{7,6},{8,7},{9,8},{10,9},{11,1... | collective-permute-start | bytes 393224 | tf_op jit(solution)/shard_map/ppermute | solution.py:15
  75.1 1.3 %fusion.45 = f32[256,512]{1,0:T(8,128)S(1)} fusion(bf16[2,512,512]{2,1,0:T(8,128)(2,1)} %param.56, f32[256,512]{1,0:T(8,128)S(1)} %multiply_add_fusion), kind=kOutput, calls=%fused_computation.72 | convolution fusion | flops 134348800 | bytes 1572864 | tf_op jit(solution)/shard_map/dot_general | solution.py:21
  76.5 1.3 %fusion.48 = f32[256,512]{1,0:T(8,128)S(1)} fusion(bf16[2,512,512]{2,1,0:T(8,128)(2,1)} %param.57, f32[256,512]{1,0:T(8,128)S(1)} %multiply_add_fusion), kind=kOutput, calls=%fused_computation.75 | convolution fusion | flops 134348800 | bytes 1572864 | tf_op jit(solution)/shard_map/dot_general | solution.py:21
  77.8 8.9 %gather_fusion.11 = f32[2048,512]{1,0:T(8,128)} fusion(f32[256,512]{1,0:T(8,128)S(1)} %fusion.45, s32[2048]{0:T(1024)S(1)} %fusion.96), kind=kCustom, calls=%fused_computation.8.clone | custom fusion | bytes 8396800 | tf_op jit(solution)/shard_map/jit(_take)/gather | solution.py:54
  86.8 9.2 %gather_fusion.10 = bf16[2048,512]{1,0:T(8,128)(2,1)} fusion(bf16[512,512]{1,0:T(8,128)(2,1)S(1)} %pad_maximum_fusion.2, s32[2048]{0:T(1024)S(1)} %fusion.95), kind=kCustom, calls=%fused_computation.7.clone | custom fusion | bytes 4202496 | tf_op jit(solution)/shard_map/jit(_take)/gather | solution.py:54
  96.0 6.3 %fusion.32 = bf16[256,512]{1,0:T(8,128)(2,1)S(1)} fusion(f32[2048,512]{1,0:T(8,128)} %gather_fusion.11, bf16[2048,512]{1,0:T(8,128)(2,1)} %gather_fusion.10, pred[2048]{0:T(1024)(128)(4,1)S(1)} %copy-done.25, pred[2048]{0:T(1024)(128)(4,1)S(1)} %copy-done.27, s32[2048]{0:T(1024)S(1)} %bitcast.119), kind=kOutput, calls=%fused_computation.54 | convolution fusion | flops 3230269440 | bytes 6565888 | tf_op jit(solution)/shard_map/dot_general | solution.py:34
  102.3 1.9 %fusion.128 = (f32[256]{0:T(256)S(1)}, f32[256,512]{1,0:T(8,128)S(1)}) fusion(bf16[2,512,512]{2,1,0:T(8,128)(2,1)} %param.59, f32[256,512]{1,0:T(8,128)S(1)} %fusion.48, bf16[256,512]{1,0:T(8,128)(2,1)S(1)} %fusion.32, bf16[2,512,512]{2,1,0:T(8,128)(2,1)} %param.58), kind=kOutput, calls=%fused_computation.204 | convolution fusion | flops 269352704 | bytes 2360320 | tf_op jit(solution)/shard_map/dot_general | solution.py:21
  104.4 1.4 %convolution_convert_fusion = bf16[256,512]{1,0:T(8,128)(2,1)S(1)} fusion(bf16[512,512]{1,0:T(8,128)(2,1)} %param.60, f32[256,512]{1,0:T(8,128)S(1)} %multiply_add_fusion, f32[256,512]{1,0:T(8,128)S(1)} %get-tuple-element.25, f32[256]{0:T(256)S(1)} %add_rsqrt_fusion, f32[256]{0:T(256)S(1)} %broadcast_multiply_fusion), kind=kOutput, calls=%fused_computation.48 | convolution fusion | flops 134873088 | bytes 1837056 | tf_op jit(solution)/shard_map/dot_general | solution.py:21
  105.8 4.5 %collective-permute-start.6 = (bf16[256,512]{1,0:T(8,128)(2,1)S(1)}, bf16[256,512]{1,0:T(8,128)(2,1)S(1)}, u32[]{:S(2)}, u32[]{:S(2)}) collective-permute-start(bf16[256,512]{1,0:T(8,128)(2,1)S(1)} %convolution_convert_fusion), channel_id=1, source_target_pairs={{0,1},{1,2},{2,3},{3,4},{4,5},{5,6},{6,7},{7,8},{8,9},{9,10},{10,1... | collective-permute-start | bytes 786440 | tf_op jit(solution)/shard_map/ppermute | solution.py:12
  110.4 1.9 %collective-permute-start.7 = (bf16[256,512]{1,0:T(8,128)(2,1)S(1)}, bf16[256,512]{1,0:T(8,128)(2,1)}, u32[]{:S(2)}, u32[]{:S(2)}) collective-permute-start(bf16[256,512]{1,0:T(8,128)(2,1)S(1)} %convolution_convert_fusion), channel_id=1, source_target_pairs={{1,0},{2,1},{3,2},{4,3},{5,4},{6,5},{7,6},{8,7},{9,8},{10,9},{11,1... | collective-permute-start | bytes 786440 | tf_op jit(solution)/shard_map/ppermute | solution.py:15
  112.3 2.2 %gather_fusion.2 = f32[768,512]{1,0:T(8,128)S(1)} fusion(f32[256,512]{1,0:T(8,128)S(1)} %fusion.132, s32[1024]{0:T(1024)S(1)} %pad_clamp_fusion), kind=kCustom, calls=%fused_computation.11 | custom fusion | bytes 3148800 | tf_op jit(solution)/shard_map/jit(_take)/gather | solution.py:42
  114.5 2.2 %fusion.131 = f32[256,512]{1,0:T(8,128)} fusion(bf16[256,512]{1,0:T(8,128)(2,1)S(1)} %multiply_convert_fusion.7, bf16[512,512]{1,0:T(8,128)(2,1)} %param.63), kind=kOutput, calls=%fused_computation.205 | convolution fusion | flops 134217728 | bytes 1310720 | tf_op jit(solution)/shard_map/dot_general | solution.py:21
  116.7 2.4 %collective-permute-done.7 = bf16[256,512]{1,0:T(8,128)(2,1)} collective-permute-done((bf16[256,512]{1,0:T(8,128)(2,1)S(1)}, bf16[256,512]{1,0:T(8,128)(2,1)}, u32[]{:S(2)}, u32[]{:S(2)}) %collective-permute-start.7) | collective-permute-done | bytes 262176 | tf_op jit(solution)/shard_map/ppermute | solution.py:15
  120.1 3.3 %gather_fusion.1 = bf16[768,512]{1,0:T(8,128)(2,1)} fusion(bf16[768,512]{1,0:T(8,128)(2,1)S(1)} %pad_maximum_fusion, s32[1024]{0:T(1024)S(1)} %copy-done.17), kind=kCustom, calls=%fused_computation.10 | custom fusion | bytes 1575936 | tf_op jit(solution)/shard_map/jit(_take)/gather | solution.py:150
  123.5 2.1 %fusion.41 = f32[768,512]{1,0:T(8,128)S(1)} fusion(bf16[512,512]{1,0:T(8,128)(2,1)S(1)} %copy-done, f32[768,512]{1,0:T(8,128)S(1)} %gather_fusion.2, bf16[768,512]{1,0:T(8,128)(2,1)} %gather_fusion.1, pred[768]{0:T(1024)(128)(4,1)S(1)} %copy-done.29, pred[768]{0:T(1024)(128)(4,1)S(1)} %copy-done.30), kind=kOutput, calls=%fused_computation.66 | convolution fusion | flops 406192128 | bytes 4457984 | tf_op jit(solution)/shard_map/dot_general | solution.py:21
  126.7 2.3 %convolution_convert_fusion.5 = bf16[256,227]{0,1:T(8,128)(2,1)} fusion(bf16[512,227]{0,1:T(8,128)(2,1)S(1)} %copy-done.32, f32[256,512]{1,0:T(8,128)S(1)} %copy-done.8, bf16[256,512]{1,0:T(8,128)(2,1)S(1)} %fusion.26, bf16[512,512]{1,0:T(8,128)(2,1)} %param.64), kind=kOutput, calls=%fused_computation.55 | convolution fusion | flops 194568960 | bytes 1659392 | tf_op jit(solution)/shard_map/dot_general | solution.py:21
  (149 shorter events, 20.9 us)
Async XLA Ops:
  0.0 123.4 %copy-start = (bf16[512,512]{1,0:T(8,128)(2,1)S(1)}, bf16[512,512]{1,0:T(8,128)(2,1)}, u32[]{:S(2)}) copy-start(bf16[512,512]{1,0:T(8,128)(2,1)} %param.62) | copy-start | bytes 1572868
  2.2 8.1 %copy-start.35 = (s32[1,128]{1,0:T(1,128)S(1)}, s32[1,128]{1,0:T(1,128)}, u32[]{:S(2)}) copy-start(s32[1,128]{1,0:T(1,128)} %param.43) | copy-start | bytes 1540
  2.2 8.7 %copy-start.11 = (s32[16,128]{1,0:T(8,128)S(1)}, s32[16,128]{1,0:T(8,128)}, u32[]{:S(2)}) copy-start(s32[16,128]{1,0:T(8,128)} %param.41) | copy-start | bytes 24580
  2.2 8.7 %copy-start.12 = (s32[16,128]{1,0:T(8,128)S(1)}, s32[16,128]{1,0:T(8,128)}, u32[]{:S(2)}) copy-start(s32[16,128]{1,0:T(8,128)} %param.42) | copy-start | bytes 24580
  2.6 9.8 %copy-start.21 = (s32[1,3,1,128]{3,2,1,0:T(1,128)S(1)}, s32[1,3,1,128]{3,2,1,0:T(1,128)}, u32[]{:S(2)}) copy-start(s32[1,3,1,128]{3,2,1,0:T(1,128)} %param.39) | copy-start | bytes 4612
  2.6 11.1 %copy-start.36 = (s32[1,3]{1,0:T(1,128)S(1)}, s32[1,3]{1,0:T(1,128)}, u32[]{:S(2)}) copy-start(s32[1,3]{1,0:T(1,128)} %param.40) | copy-start | bytes 40
  2.6 11.6 %copy-start.33 = (f32[3,512]{1,0:T(4,128)S(1)}, f32[3,512]{1,0:T(4,128)}, u32[]{:S(2)}) copy-start(f32[3,512]{1,0:T(4,128)} %param.48) | copy-start | bytes 18436
  2.6 11.6 %copy-start.34 = (f32[3,256]{1,0:T(4,128)S(1)}, f32[3,256]{1,0:T(4,128)}, u32[]{:S(2)}) copy-start(f32[3,256]{1,0:T(4,128)} %param.37) | copy-start | bytes 9220
  3.6 18.9 %collective-permute-start = (bf16[128,512]{1,0:T(8,128)(2,1)S(1)}, bf16[128,512]{1,0:T(8,128)(2,1)}, u32[]{:S(2)}, u32[]{:S(2)}) collective-permute-start(bf16[128,512]{1,0:T(8,128)(2,1)S(1)} %broadcast_select_fusion.3), channel_id=1, source_target_pairs={{0,1},{1,2},{2,3},{3,4},{4,5},{5,6},{6,7},{7,8},{8,9},{9,10},{10,1... | collective-permute-start | bytes 393224 | tf_op jit(solution)/shard_map/ppermute | solution.py:12
  8.2 6.8 %copy-start.3 = (bf16[512,512]{1,0:T(8,128)(2,1)S(1)}, bf16[512,512]{1,0:T(8,128)(2,1)}, u32[]{:S(2)}) copy-start(bf16[512,512]{1,0:T(8,128)(2,1)} %param.50) | copy-start | bytes 1572868
  8.3 14.2 %collective-permute-start.1 = (bf16[128,512]{1,0:T(8,128)(2,1)S(1)}, bf16[128,512]{1,0:T(8,128)(2,1)}, u32[]{:S(2)}, u32[]{:S(2)}) collective-permute-start(bf16[128,512]{1,0:T(8,128)(2,1)S(1)} %broadcast_select_fusion.2), channel_id=1, source_target_pairs={{1,0},{2,1},{3,2},{4,3},{5,4},{6,5},{7,6},{8,7},{9,8},{10,9},{11,1... | collective-permute-start | bytes 393224 | tf_op jit(solution)/shard_map/ppermute | solution.py:15
  12.4 2.9 %copy-start.4 = (bf16[512,512]{1,0:T(8,128)(2,1)S(1)}, bf16[512,512]{1,0:T(8,128)(2,1)}, u32[]{:S(2)}) copy-start(bf16[512,512]{1,0:T(8,128)(2,1)} %param.52) | copy-start | bytes 1572868
  13.1 3.3 %copy-start.15 = (s32[3,128]{1,0:T(4,128)}, s32[3,128]{1,0:T(4,128)S(1)}, u32[]{:S(2)}) copy-start(s32[3,128]{1,0:T(4,128)S(1)} %reduce) | copy-start | bytes 4612
  30.3 18.1 %collective-permute-start.2 = (bf16[128,512]{1,0:T(8,128)(2,1)S(1)}, bf16[128,512]{1,0:T(8,128)(2,1)S(1)}, u32[]{:S(2)}, u32[]{:S(2)}) collective-permute-start(bf16[128,512]{1,0:T(8,128)(2,1)S(1)} %broadcast_select_fusion.1), channel_id=1, source_target_pairs={{0,1},{1,2},{2,3},{3,4},{4,5},{5,6},{6,7},{7,8},{8,9},{9,10},{10,1... | collective-permute-start | bytes 393224 | tf_op jit(solution)/shard_map/ppermute | solution.py:12
  34.9 13.5 %collective-permute-start.3 = (bf16[128,512]{1,0:T(8,128)(2,1)S(1)}, bf16[128,512]{1,0:T(8,128)(2,1)S(1)}, u32[]{:S(2)}, u32[]{:S(2)}) collective-permute-start(bf16[128,512]{1,0:T(8,128)(2,1)S(1)} %broadcast_select_fusion.1), channel_id=1, source_target_pairs={{1,0},{2,1},{3,2},{4,3},{5,4},{6,5},{7,6},{8,7},{9,8},{10,9},{11,1... | collective-permute-start | bytes 393224 | tf_op jit(solution)/shard_map/ppermute | solution.py:15
  48.4 9.2 %copy-start.13 = (s32[16,128]{1,0:T(8,128)S(1)}, s32[16,128]{1,0:T(8,128)}, u32[]{:S(2)}) copy-start(s32[16,128]{1,0:T(8,128)} %param.42) | copy-start | bytes 24580
  48.4 9.2 %copy-start.24 = (pred[2048]{0:T(1024)(128)(4,1)S(1)}, pred[2048]{0:T(1024)(128)(4,1)}, u32[]{:S(2)}) copy-start(pred[2048]{0:T(1024)(128)(4,1)} %get-tuple-element.26) | copy-start | bytes 6148
  48.5 9.2 %copy-start.26 = (pred[2048]{0:T(1024)(128)(4,1)S(1)}, pred[2048]{0:T(1024)(128)(4,1)}, u32[]{:S(2)}) copy-start(pred[2048]{0:T(1024)(128)(4,1)} %get-tuple-element.27) | copy-start | bytes 6148
  68.5 18.2 %collective-permute-start.4 = (bf16[128,512]{1,0:T(8,128)(2,1)S(1)}, bf16[128,512]{1,0:T(8,128)(2,1)S(1)}, u32[]{:S(2)}, u32[]{:S(2)}) collective-permute-start(bf16[128,512]{1,0:T(8,128)(2,1)S(1)} %broadcast_select_fusion), channel_id=1, source_target_pairs={{0,1},{1,2},{2,3},{3,4},{4,5},{5,6},{6,7},{7,8},{8,9},{9,10},{10,1... | collective-permute-start | bytes 393224 | tf_op jit(solution)/shard_map/ppermute | solution.py:12
  73.0 13.7 %collective-permute-start.5 = (bf16[128,512]{1,0:T(8,128)(2,1)S(1)}, bf16[128,512]{1,0:T(8,128)(2,1)S(1)}, u32[]{:S(2)}, u32[]{:S(2)}) collective-permute-start(bf16[128,512]{1,0:T(8,128)(2,1)S(1)} %broadcast_select_fusion), channel_id=1, source_target_pairs={{1,0},{2,1},{3,2},{4,3},{5,4},{6,5},{7,6},{8,7},{9,8},{10,9},{11,1... | collective-permute-start | bytes 393224 | tf_op jit(solution)/shard_map/ppermute | solution.py:15
  86.8 9.2 %copy-start.14 = (s32[16,128]{1,0:T(8,128)S(1)}, s32[16,128]{1,0:T(8,128)}, u32[]{:S(2)}) copy-start(s32[16,128]{1,0:T(8,128)} %param.42) | copy-start | bytes 24580
  86.8 9.2 %copy-start.25 = (pred[2048]{0:T(1024)(128)(4,1)S(1)}, pred[2048]{0:T(1024)(128)(4,1)}, u32[]{:S(2)}) copy-start(pred[2048]{0:T(1024)(128)(4,1)} %get-tuple-element.26) | copy-start | bytes 6148
  86.8 9.2 %copy-start.27 = (pred[2048]{0:T(1024)(128)(4,1)S(1)}, pred[2048]{0:T(1024)(128)(4,1)}, u32[]{:S(2)}) copy-start(pred[2048]{0:T(1024)(128)(4,1)} %get-tuple-element.27) | copy-start | bytes 6148
  104.2 8.1 %copy-start.18 = (s32[768]{0:T(1024)S(1)}, s32[768]{0:T(1024)}, u32[]{:S(2)}) copy-start(s32[768]{0:T(1024)} %fusion.98) | copy-start | bytes 9220
  104.2 8.1 %copy-start.31 = (pred[3,256]{1,0:T(4,128)(4,1)S(1)}, pred[3,256]{1,0:T(4,128)(4,1)}, u32[]{:S(2)}) copy-start(pred[3,256]{1,0:T(4,128)(4,1)} %iota_compare_fusion.11) | copy-start | bytes 2308
  105.8 10.9 %collective-permute-start.6 = (bf16[256,512]{1,0:T(8,128)(2,1)S(1)}, bf16[256,512]{1,0:T(8,128)(2,1)S(1)}, u32[]{:S(2)}, u32[]{:S(2)}) collective-permute-start(bf16[256,512]{1,0:T(8,128)(2,1)S(1)} %convolution_convert_fusion), channel_id=1, source_target_pairs={{0,1},{1,2},{2,3},{3,4},{4,5},{5,6},{6,7},{7,8},{8,9},{9,10},{10,1... | collective-permute-start | bytes 786440 | tf_op jit(solution)/shard_map/ppermute | solution.py:12
  110.4 8.7 %collective-permute-start.7 = (bf16[256,512]{1,0:T(8,128)(2,1)S(1)}, bf16[256,512]{1,0:T(8,128)(2,1)}, u32[]{:S(2)}, u32[]{:S(2)}) collective-permute-start(bf16[256,512]{1,0:T(8,128)(2,1)S(1)} %convolution_convert_fusion), channel_id=1, source_target_pairs={{1,0},{2,1},{3,2},{4,3},{5,4},{6,5},{7,6},{8,7},{9,8},{10,9},{11,1... | collective-permute-start | bytes 786440 | tf_op jit(solution)/shard_map/ppermute | solution.py:15
  114.5 5.6 %copy-start.17 = (s32[1024]{0:T(1024)S(1)}, s32[1024]{0:T(1024)}, u32[]{:S(2)}) copy-start(s32[1024]{0:T(1024)} %pad_clamp_fusion.1) | copy-start | bytes 12292
  120.1 3.3 %copy-start.29 = (pred[768]{0:T(1024)(128)(4,1)S(1)}, pred[768]{0:T(1024)(128)(4,1)}, u32[]{:S(2)}) copy-start(pred[768]{0:T(1024)(128)(4,1)} %get-tuple-element.28) | copy-start | bytes 2308
  120.1 3.3 %copy-start.30 = (pred[768]{0:T(1024)(128)(4,1)S(1)}, pred[768]{0:T(1024)(128)(4,1)}, u32[]{:S(2)}) copy-start(pred[768]{0:T(1024)(128)(4,1)} %get-tuple-element.29) | copy-start | bytes 2308
  123.4 3.3 %copy-start.8 = (f32[256,512]{1,0:T(8,128)S(1)}, f32[256,512]{1,0:T(8,128)}, u32[]{:S(2)}) copy-start(f32[256,512]{1,0:T(8,128)} %fusion.131) | copy-start | bytes 1572868
  123.5 3.3 %copy-start.32 = (bf16[512,227]{0,1:T(8,128)(2,1)S(1)}, bf16[512,227]{0,1:T(8,128)(2,1)}, u32[]{:S(2)}) copy-start(bf16[512,227]{0,1:T(8,128)(2,1)} %param.65) | copy-start | bytes 697348
  (14 other events, 28.7 us)
where the time goes:
time: 130 us; the launch traced here: 129 us
  local copies, waits for them, and re-layouts  49.9 us (38%)
  matrix products  39.9 us (31%)
  starting transfers between devices  25.3 us (19%)
  other arithmetic  10.6 us (8%)
  waiting for transfers between devices  2.41 us (2%)
    dot_general x19, matrix products, product(): return jnp.dot(left, right, preferred_element_type=jnp.float32)  24.8 us
    gather x2, local copies, waits for them, and re-layouts, mesh_sum(): jnp.take(table, senders.reshape(-1), axis=0).astype(jnp.float32)  18.4 us
    gather x2, local copies, waits for them, and re-layouts, mesh_sum(): jnp.take(target, flat_in, axis=0)  17.8 us
    ppermute x4, starting transfers between devices, with_halo(): lax.ppermute(lax.slice_in_dim(block, block.shape[dim] - width, None, axis...  17.3 us
    dot_general x4, matrix products, onehot_sum(): jnp.dot(selector, message, precision=lax.Precision.HIGHEST, preferred_ele...  14.4 us
    ppermute x4, starting transfers between devices, with_halo(): lax.ppermute(lax.slice_in_dim(block, 0, width, axis=dim), axis, backward)  8 us
    gather x2, local copies, waits for them, and re-layouts, edge_messages(): jnp.take(target, flat_in, axis=0)  3.91 us
    gather x1, local copies, waits for them, and re-layouts, body(): jnp.take(table, shifted.reshape(-1), axis=0).reshape(3, dec_width, -1)  3.32 us
  transfers between devices with their start and end apart: 8, of which 1 were waited for; matrix products, arithmetic and copies ran while one was open for 31% of the time, Pallas kernels for 0%

commit v1 on v0

v1 whole, which is shorter than its diff:
```python
import functools

import jax
import jax.numpy as jnp
from jax import lax
from jax.experimental import pallas as pl
from jax.experimental.pallas import tpu as pltpu
from jax.sharding import PartitionSpec as P

MESH = pl.DeviceIdType.MESH
BF = jnp.bfloat16
F32 = jnp.float32
LANES = 128


def product(left, right):
    return jnp.dot(left, right, preferred_element_type=F32)


def product_nt(left, right):
    return lax.dot_general(left, right, (((1,), (1,)), ((), ())), preferred_element_type=F32)


def product_tn(left, right):
    return lax.dot_general(left, right, (((0,), (0,)), ((), ())), preferred_element_type=F32)


def silu(x):
    half = 0.5 * x
    return half + half * jnp.tanh(half)


def norm_rows(values):
    centre = values - jnp.mean(values, axis=-1, keepdims=True)
    spread = jnp.mean(centre * centre, axis=-1, keepdims=True)
    return centre * lax.rsqrt(spread + 1e-05)


def hot_columns(column, width):
    ids = lax.broadcasted_iota(jnp.int32, (column.shape[0], width), 1).astype(F32)
    return jnp.where(column == ids, 1.0, 0.0).astype(BF)


def hot_rows(row, height):
    ids = lax.broadcasted_iota(jnp.int32, (height, row.shape[1]), 0).astype(F32)
    return jnp.where(row == ids, 1.0, 0.0).astype(BF)


def kernel(
    n,
    state_t,
    static,
    enc_send,
    enc_recv,
    enc_counts,
    mesh_send,
    mesh_recv,
    halo,
    dec_send,
    dec_recv,
    dec_counts,
    grid_embed,
    mesh_embed,
    readout_t,
    w_es,
    w_et,
    w_em,
    w_er,
    w_ea,
    w_ef,
    w_ps,
    w_pt,
    w_pr,
    w_pa,
    w_pf,
    w_ds,
    w_dt,
    w_dm,
    w_dr,
    w_da,
    out,
    weights,
    id_rows,
    id_cols,
    enc_leave,
    enc_table,
    rim,
    tables,
    dec_table,
    grid_tgt,
    hot_mesh,
    sel_mesh,
    hot_dec,
    sel_dec,
    hidden,
    weight_sem,
    send_sem,
    recv_sem,
):
    layers = w_ps.shape[0]
    nodes = static.shape[1]
    cells = state_t.shape[1]
    width_e = enc_send.shape[2] * LANES
    blocks_d = dec_send.shape[2]
    width_d = blocks_d * LANES
    rim_w = halo.shape[1]
    blocks_m = mesh_send.shape[0]
    ext_w = nodes + 2 * rim_w

    me = lax.axis_index("band")
    left = lax.rem(me + n - 1, n)
    right = lax.rem(me + 1, n)
    has_left = me > 0
    has_right = me < n - 1

    barrier = pltpu.get_barrier_semaphore()

    @pl.when(has_left)
    def _():
        pl.semaphore_signal(barrier, inc=1, device_id={"band": left}, device_id_type=MESH)

    @pl.when(has_right)
    def _():
        pl.semaphore_signal(barrier, inc=1, device_id={"band": right}, device_id_type=MESH)

    order = [w_es, w_et, w_er, w_em, w_ea, w_ef]
    names = ["es", "et", "er", "em", "ea", "ef"]
    for l in range(layers):
        order += [w.at[l] for w in (w_ps, w_pt, w_pr, w_pa, w_pf)]
        names += [a + str(l) for a in ("ps", "pt", "pr", "pa", "pf")]
    order += [w_ds, w_dt, w_dr, w_dm, w_da]
    names += ["ds", "dt", "dr", "dm", "da"]
    copies = {}
    for k, (name, ref) in enumerate(zip(names, order)):
        copy = pltpu.make_async_copy(ref, weights.at[k], weight_sem.at[k])
        copy.start()
        copies[name] = (copy, k)

    def weight(name):
        copy, k = copies[name]
        copy.wait()
        return weights[k]

    def to_left(r, src, dst):
        return pltpu.make_async_remote_copy(
            src_ref=src, dst_ref=dst, send_sem=send_sem.at[2 * r], recv_sem=recv_sem.at[2 * r],
            device_id={"band": left}, device_id_type=MESH)

    def to_right(r, src, dst):
        return pltpu.make_async_remote_copy(
            src_ref=src, dst_ref=dst, send_sem=send_sem.at[2 * r + 1],
            recv_sem=recv_sem.at[2 * r + 1], device_id={"band": right}, device_id_type=MESH)

    sent = []

    def exchange(r, src_left, src_right, low, high):
        one, two = to_left(r, src_left, high), to_right(r, src_right, low)

        @pl.when(has_left)
        def _():
            one.start()

        @pl.when(has_right)
        def _():
            two.start()

        sent.append((one, two))

    def arrive(r):
        one, two = sent[r]

        @pl.when(has_left)
        def _():
            two.wait_recv()

        @pl.when(has_right)
        def _():
            one.wait_recv()

    lows = [enc_table.at[0]]
    highs = [enc_table.at[2]]
    for l in range(layers):
        lows.append(tables.at[l, pl.ds(0, rim_w)])
        highs.append(tables.at[l, pl.ds(rim_w + nodes, rim_w)])
    lows.append(dec_table.at[0])
    highs.append(dec_table.at[2])

    @pl.when(jnp.logical_not(has_left))
    def _():
        for ref in lows:
            ref[...] = jnp.zeros(ref.shape, BF)

    @pl.when(jnp.logical_not(has_right))
    def _():
        for ref in highs:
            ref[...] = jnp.zeros(ref.shape, BF)

    id_rows[...] = jnp.zeros(id_rows.shape, F32)
    base_ms, base_mr = 0, blocks_m
    base_h = 2 * blocks_m
    base_es = base_h + 8
    base_er = base_es + 8
    base_ds = base_er + 8
    base_dr = base_ds + 8
    id_rows[base_ms:base_ms + blocks_m, :] = mesh_send[...].astype(F32)
    id_rows[base_mr:base_mr + blocks_m, :] = mesh_recv[...].astype(F32)
    id_rows[base_h:base_h + 1, :] = halo[...].astype(F32)
    for o in range(3):
        id_rows[base_es + o:base_es + o + 1, :] = enc_send[0, o].astype(F32)
        id_rows[base_er + o:base_er + o + 1, :] = enc_recv[0, o].astype(F32)
        id_rows[base_ds + 2 * o:base_ds + 2 * o + 2, :] = dec_send[0, o].astype(F32)
        id_rows[base_dr + 2 * o:base_dr + 2 * o + 2, :] = dec_recv[0, o].astype(F32)
    id_cols[...] = id_rows[...].T

    def column(j):
        return id_cols[:, j:j + 1]

    latent = norm_rows(silu(product_tn(state_t[...], grid_embed[...]))).astype(BF)
    grid_source = product(latent, weight("es")).astype(BF)
    for o in range(3):
        rows = product(hot_columns(column(base_es + o), cells), grid_source).astype(BF)
        if o == 1:
            enc_table[1] = rows
        else:
            enc_leave[o // 2] = rows
    pl.semaphore_wait(barrier, has_left.astype(jnp.int32) + has_right.astype(jnp.int32))
    exchange(0, enc_leave.at[0], enc_leave.at[1], enc_table.at[0], enc_table.at[2])

    static_t = jnp.concatenate([static[...], jnp.zeros((5, nodes), F32)], axis=0).T
    total = static_t[:, 0:1] * mesh_embed[0:1, :]
    for f in range(1, static.shape[0]):
        total = total + static_t[:, f:f + 1] * mesh_embed[f:f + 1, :]
    mesh_state = silu(total)
    mesh_low = mesh_state.astype(BF)
    target = product(mesh_low, weight("et")).astype(BF)
    kept = product(mesh_low, weight("er"))
    sel = []
    lane = lax.broadcasted_iota(jnp.int32, (1, LANES), 1)
    for o in range(3):
        live = lane < enc_counts[0, o]
        sel.append(hot_rows(jnp.where(live, id_rows[base_er + o:base_er + o + 1, :], -1.0), nodes))

    hot_halo = hot_columns(column(base_h), nodes)
    for j in range(blocks_m):
        at = slice(j * LANES, (j + 1) * LANES)
        hot_mesh[at, 0:ext_w] = hot_columns(column(base_ms + j), ext_w)
        hot_mesh[at, ext_w:ext_w + nodes] = hot_columns(column(base_mr + j), nodes)
        sel_mesh[:, at] = hot_rows(id_rows[base_mr + j:base_mr + j + 1, :], nodes)
    for o in range(3):
        for b in range(blocks_d):
            j = o * blocks_d + b
            at = slice(j * LANES, (j + 1) * LANES)
            hot_dec[at, 0:nodes] = hot_columns(column(base_ds + j), nodes)
            hot_dec[at, nodes:nodes + cells] = hot_columns(column(base_dr + j), cells)
            live = lane + b * LANES < dec_counts[0, o]
            row = jnp.where(live, id_rows[base_dr + j:base_dr + j + 1, :], -1.0)
            sel_dec[:, at] = hot_rows(row, cells)

    arrive(0)
    for o in range(3):
        joined = enc_table[o].astype(F32) + product(hot_columns(column(base_er + o), nodes), target)
        hidden[o * width_e:(o + 1) * width_e, :] = silu(joined).astype(BF)
    summed = product(jnp.concatenate(sel, axis=1), hidden[0:3 * width_e, :]).astype(BF)
    summed = product(summed, weight("em")).astype(BF)
    inner = silu(kept + product(summed, weight("ea"))).astype(BF)
    mesh_state = mesh_state + norm_rows(product(inner, weight("ef")))

    chunk = 512
    for l in range(layers):
        tag = str(l)
        mesh_low = mesh_state.astype(BF)
        source = product(mesh_low, weight("ps" + tag)).astype(BF)
        rim[l] = product(hot_halo, source).astype(BF)
        exchange(1 + l, rim.at[l], rim.at[l], lows[1 + l], highs[1 + l])
        tables[l, rim_w:rim_w + nodes, :] = source
        tables[l, ext_w:ext_w + nodes, :] = product(mesh_low, weight("pt" + tag)).astype(BF)
        kept = product(mesh_low, weight("pr" + tag))
        if l == 0:
            grid_tgt[...] = product(latent, weight("dt")).astype(BF)
            grid_kept = product(latent, weight("dr"))
        arrive(1 + l)
        for c in range(blocks_m * LANES // chunk):
            at = slice(c * chunk, (c + 1) * chunk)
            hidden[at, :] = silu(product(hot_mesh[at, :], tables[l])).astype(BF)
        summed = product(sel_mesh[...], hidden[...]).astype(BF)
        inner = silu(kept + product(summed, weight("pa" + tag))).astype(BF)
        mesh_state = mesh_state + norm_rows(product(inner, weight("pf" + tag)))

    dec_table[1] = product(mesh_state.astype(BF), weight("ds")).astype(BF)
    exchange(1 + layers, dec_table.at[1], dec_table.at[1], dec_table.at[0], dec_table.at[2])

    def decode(o):
        at = slice(o * width_d, (o + 1) * width_d)
        joined = product(hot_dec[at, 0:nodes], dec_table[o]) + product(
            hot_dec[at, nodes:nodes + cells], grid_tgt[...])
        hidden[at, :] = silu(joined).astype(BF)

    decode(1)
    arrive(1 + layers)
    decode(0)
    decode(2)
    summed = product(sel_dec[...], hidden[0:3 * width_d, :]).astype(BF)
    summed = product(summed, weight("dm")).astype(BF)
    inner = silu(grid_kept + product(summed, weight("da"))).astype(BF)
    out[...] = product_nt(readout_t[...], inner).astype(BF)

    for one, two in sent:
        @pl.when(has_left)
        def _(one=one):
            one.wait_send()

        @pl.when(has_right)
        def _(two=two):
            two.wait_send()


def body(
    n,
    grid_state,
    mesh_static,
    encoder_senders,
    encoder_receivers,
    encoder_counts,
    mesh_senders,
    mesh_receivers,
    halo_rows,
    backward_icosa_emitters,
    backward_cell_destination,
    backward_active_slot_amounts,
    grid_embed,
    mesh_embed,
    encoder_source,
    encoder_target,
    encoder_message,
    encoder_retain,
    encoder_absorb,
    encoder_finish,
    process_source,
    process_target,
    process_retain,
    process_absorb,
    process_finish,
    decoder_source,
    decoder_target,
    decoder_message,
    decoder_retain,
    decoder_absorb,
    readout_matrix,
):
    cells = grid_state.shape[0]
    nodes = mesh_static.shape[1]
    dim = grid_embed.shape[1]
    layers = process_source.shape[0]
    rim_w = halo_rows.shape[1]
    edges = mesh_senders.size
    width_e = encoder_senders.size // 3
    width_d = backward_icosa_emitters.size // 3
    n_weights = 11 + 5 * layers
    rounds = 2 + layers
    vmem = pl.BlockSpec(memory_space=pltpu.VMEM)
    smem = pl.BlockSpec(memory_space=pltpu.SMEM)
    far = pl.BlockSpec(memory_space=pl.ANY)
    out_t = pl.pallas_call(
        functools.partial(kernel, n),
        out_shape=jax.ShapeDtypeStruct((readout_matrix.shape[1], cells), BF),
        in_specs=[vmem] * 4 + [smem] + [vmem] * 5 + [smem] + [vmem] * 3 + [far] * 16,
        out_specs=vmem,
        scratch_shapes=[
            pltpu.VMEM((n_weights, dim, dim), BF),
            pltpu.VMEM((LANES, LANES), F32),
            pltpu.VMEM((LANES, LANES), F32),
            pltpu.VMEM((2, width_e, dim), BF),
            pltpu.VMEM((3, width_e, dim), BF),
            pltpu.VMEM((layers, rim_w, dim), BF),
            pltpu.VMEM((layers, 2 * rim_w + 2 * nodes, dim), BF),
            pltpu.VMEM((3, nodes, dim), BF),
            pltpu.VMEM((cells, dim), BF),
            pltpu.VMEM((edges, 2 * rim_w + 2 * nodes), BF),
            pltpu.VMEM((nodes, edges), BF),
            pltpu.VMEM((3 * width_d, nodes + cells), BF),
            pltpu.VMEM((cells, 3 * width_d), BF),
            pltpu.VMEM((edges, dim), BF),
            pltpu.SemaphoreType.DMA((n_weights,)),
            pltpu.SemaphoreType.DMA((2 * rounds,)),
            pltpu.SemaphoreType.DMA((2 * rounds,)),
        ],
        compiler_params=pltpu.CompilerParams(
            collective_id=0, has_side_effects=True, vmem_limit_bytes=56 * 1024 * 1024
        ),
    )(
        grid_state.T,
        mesh_static,
        encoder_senders,
        encoder_receivers,
        encoder_counts,
        mesh_senders,
        mesh_receivers,
        halo_rows,
        backward_icosa_emitters,
        backward_cell_destination,
        backward_active_slot_amounts,
        grid_embed,
        mesh_embed,
        readout_matrix.T,
        encoder_source,
        encoder_target,
        encoder_message,
        encoder_retain,
        encoder_absorb,
        encoder_finish,
        process_source,
        process_target,
        process_retain,
        process_absorb,
        process_finish,
        decoder_source,
        decoder_target,
        decoder_message,
        decoder_retain,
        decoder_absorb,
    )
    return out_t.T


def solution(mesh):
    placed = (
        P(("groups", "band"), None),
        P(None, "band"),
        P("band", None, None, None),
        P("band", None, None, None),
        P("band", None),
        P("band", None),
        P("band", None),
        P("band", None),
        P("band", None, None, None),
        P("band", None, None, None),
        P("band", None),
    ) + (P(),) * 19
    return jax.shard_map(
        functools.partial(body, mesh.shape["band"]),
        mesh=mesh,
        in_specs=placed,
        out_specs=P(("groups", "band"), None),
        check_vma=False,
    )
```

time: 130 us -> 37.9 us (0.29)
  the two profiles are of different devices: /device:TPU:13 before, /device:TPU:14 now
where the time goes in v1:
time: 37.9 us; the launch traced here: 37.7 us
  Pallas kernels  36.1 us (95%)
  local copies, waits for them, and re-layouts  1.56 us (4%)
    pallas_call x1, Pallas kernels, body(): pl.pallas_call(functools.partial(kernel, n), out_shape=jax.ShapeDtypeStru...  36.1 us
    unnamed x1, local copies, waits for them, and re-layouts  1.56 us

profile of v1, /device:TPU:14, one launch (start us, length us, event | category | flops | bytes accessed | tf_op | source)
XLA Modules:
  0.0 37.7 jit_solution(2806694856417748953)
XLA Ops:
  0.0 36.1 %shard_map.280 = bf16[227,256]{1,0:T(8,128)(2,1)} custom-call(bf16[474,256]{1,0:T(8,128)(2,1)} %bitcast.4, f32[3,256]{1,0:T(4,128)} %static.1, s32[1,3,1,128]{3,2,1,0:T(1,128)} %enc_send.1, s32[1,3,1,128]{3,2,1,0:T(1,128)} %enc_recv.1, s32[1,3]{1,0:T(1,128)} %enc_counts.1, s32[16,128]{1,0:T(8,128)} %mesh_send.1, s32[16,128]{1,0:T(8,128)} %mesh_recv.1, ...), custom_call_target="tpu_custom_call" | custom-call | tf_op jit(solution)/shard_map/pallas_call | solution.py:363
  36.1 1.6 %copy.32 = bf16[256,227]{0,1:T(8,128)(2,1)} copy(bf16[256,227]{0,1:T(8,128)(2,1)} %bitcast.3) | data formatting | bytes 232448

commit v2 on v1

--- a/solution.py
+++ b/solution.py
@@ -36,8 +36,8 @@
     return centre * lax.rsqrt(spread + 1e-05)
 
 
-def hot_columns(column, width):
-    ids = lax.broadcasted_iota(jnp.int32, (column.shape[0], width), 1).astype(F32)
+def hot_columns(column, width, first=0):
+    ids = (lax.broadcasted_iota(jnp.int32, (column.shape[0], width), 1) + first).astype(F32)
     return jnp.where(column == ids, 1.0, 0.0).astype(BF)
 
 
@@ -84,9 +84,13 @@
     id_cols,
     enc_leave,
     enc_table,
+    pre_enc,
     rim,
-    tables,
+    rim_table,
+    own_table,
+    pre_mesh,
     dec_table,
+    pre_dec,
     grid_tgt,
     hot_mesh,
     sel_mesh,
@@ -123,8 +127,8 @@
     def _():
         pl.semaphore_signal(barrier, inc=1, device_id={"band": right}, device_id_type=MESH)
 
-    order = [w_es, w_et, w_er, w_em, w_ea, w_ef]
-    names = ["es", "et", "er", "em", "ea", "ef"]
+    order = [w_es, w_et, w_em, w_ea, w_er, w_ef]
+    names = ["es", "et", "em", "ea", "er", "ef"]
     for l in range(layers):
         order += [w.at[l] for w in (w_ps, w_pt, w_pr, w_pa, w_pf)]
         names += [a + str(l) for a in ("ps", "pt", "pr", "pa", "pf")]
@@ -141,20 +145,29 @@
         copy.wait()
         return weights[k]
 
-    def to_left(r, src, dst):
+    dim = weights.shape[-1]
+    half = dim // 2
+    cols = [slice(0, half), slice(half, dim)]
+
+    def to_side(k, src, dst, side):
         return pltpu.make_async_remote_copy(
-            src_ref=src, dst_ref=dst, send_sem=send_sem.at[2 * r], recv_sem=recv_sem.at[2 * r],
-            device_id={"band": left}, device_id_type=MESH)
-
-    def to_right(r, src, dst):
-        return pltpu.make_async_remote_copy(
-            src_ref=src, dst_ref=dst, send_sem=send_sem.at[2 * r + 1],
-            recv_sem=recv_sem.at[2 * r + 1], device_id={"band": right}, device_id_type=MESH)
-
-    sent = []
-
-    def exchange(r, src_left, src_right, low, high):
-        one, two = to_left(r, src_left, high), to_right(r, src_right, low)
+            src_ref=src, dst_ref=dst, send_sem=send_sem.at[k], recv_sem=recv_sem.at[k],
+            device_id={"band": side}, device_id_type=MESH)
+
+    lows, highs = {}, {}
+    for h in range(2):
+        lows[0, h], highs[0, h] = enc_table.at[h, 0], enc_table.at[h, 1]
+        for l in range(layers):
+            lows[1 + l, h] = rim_table.at[l, h, pl.ds(0, rim_w)]
+            highs[1 + l, h] = rim_table.at[l, h, pl.ds(rim_w, rim_w)]
+        lows[1 + layers, h], highs[1 + layers, h] = dec_table.at[h, 0], dec_table.at[h, 1]
+
+    sent = {}
+
+    def exchange(r, h, src_left, src_right):
+        k = 2 * (2 * r + h)
+        one = to_side(k, src_left, highs[r, h], left)
+        two = to_side(k + 1, src_right, lows[r, h], right)
 
         @pl.when(has_left)
         def _():
@@ -164,10 +177,10 @@
         def _():
             two.start()
 
-        sent.append((one, two))
-
-    def arrive(r):
-        one, two = sent[r]
+        sent[r, h] = (one, two)
+
+    def arrive(r, h):
+        one, two = sent[r, h]
 
         @pl.when(has_left)
         def _():
@@ -177,22 +190,14 @@
         def _():
             one.wait_recv()
 
-    lows = [enc_table.at[0]]
-    highs = [enc_table.at[2]]
-    for l in range(layers):
-        lows.append(tables.at[l, pl.ds(0, rim_w)])
-        highs.append(tables.at[l, pl.ds(rim_w + nodes, rim_w)])
-    lows.append(dec_table.at[0])
-    highs.append(dec_table.at[2])
-
     @pl.when(jnp.logical_not(has_left))
     def _():
-        for ref in lows:
+        for ref in lows.values():
             ref[...] = jnp.zeros(ref.shape, BF)
 
     @pl.when(jnp.logical_not(has_right))
     def _():
-        for ref in highs:
+        for ref in highs.values():
             ref[...] = jnp.zeros(ref.shape, BF)
 
     id_rows[...] = jnp.zeros(id_rows.shape, F32)
@@ -216,15 +221,18 @@
         return id_cols[:, j:j + 1]
 
     latent = norm_rows(silu(product_tn(state_t[...], grid_embed[...]))).astype(BF)
-    grid_source = product(latent, weight("es")).astype(BF)
-    for o in range(3):
-        rows = product(hot_columns(column(base_es + o), cells), grid_source).astype(BF)
-        if o == 1:
-            enc_table[1] = rows
-        else:
-            enc_leave[o // 2] = rows
-    pl.semaphore_wait(barrier, has_left.astype(jnp.int32) + has_right.astype(jnp.int32))
-    exchange(0, enc_leave.at[0], enc_leave.at[1], enc_table.at[0], enc_table.at[2])
+    w = weight("es")
+    hot_left = hot_columns(column(base_es), cells)
+    hot_right = hot_columns(column(base_es + 2), cells)
+    hot_own = hot_columns(column(base_es + 1), cells)
+    grid_source = []
+    for h in range(2):
+        grid_source.append(product(latent, w[:, cols[h]]).astype(BF))
+        enc_leave[h, 0] = product(hot_left, grid_source[h]).astype(BF)
+        enc_leave[h, 1] = product(hot_right, grid_source[h]).astype(BF)
+        if h == 0:
+            pl.semaphore_wait(barrier, has_left.astype(jnp.int32) + has_right.astype(jnp.int32))
+        exchange(0, h, enc_leave.at[h, 0], enc_leave.at[h, 1])
 
     static_t = jnp.concatenate([static[...], jnp.zeros((5, nodes), F32)], axis=0).T
     total = static_t[:, 0:1] * mesh_embed[0:1, :]
@@ -233,78 +241,118 @@
     mesh_state = silu(total)
     mesh_low = mesh_state.astype(BF)
     target = product(mesh_low, weight("et")).astype(BF)
-    kept = product(mesh_low, weight("er"))
-    sel = []
     lane = lax.broadcasted_iota(jnp.int32, (1, LANES), 1)
-    for o in range(3):
+    sel = {}
+    for o in (1, 0, 2):
         live = lane < enc_counts[0, o]
-        sel.append(hot_rows(jnp.where(live, id_rows[base_er + o:base_er + o + 1, :], -1.0), nodes))
+        sel[o] = hot_rows(jnp.where(live, id_rows[base_er + o:base_er + o + 1, :], -1.0), nodes)
+        joined = product(hot_columns(column(base_er + o), nodes), target)
+        if o != 1:
+            pre_enc[o // 2] = joined
+    sel_side = jnp.concatenate([sel[0], sel[2]], axis=1)
+    summed_own = []
+    for h in range(2):
+        rows = product(hot_own, grid_source[h]).astype(BF).astype(F32)
+        own_hidden = silu(rows + product(hot_columns(column(base_er + 1), nodes), target[:, cols[h]]))
+        summed_own.append(product(sel[1], own_hidden.astype(BF)))
+
+    def join_weights(name_message, name_absorb):
+        return product(weight(name_message), weight(name_absorb)).astype(BF)
+
+    message_absorb = join_weights("em", "ea")
+    acc = product(mesh_low, weight("er"))
 
     hot_halo = hot_columns(column(base_h), nodes)
     for j in range(blocks_m):
         at = slice(j * LANES, (j + 1) * LANES)
-        hot_mesh[at, 0:ext_w] = hot_columns(column(base_ms + j), ext_w)
+        ids = column(base_ms + j)
+        hot_mesh[at, 0:rim_w] = hot_columns(ids, rim_w)
+        hot_mesh[at, rim_w:2 * rim_w] = hot_columns(ids, rim_w, rim_w + nodes)
+        hot_mesh[at, 2 * rim_w:ext_w] = hot_columns(ids, nodes, rim_w)
         hot_mesh[at, ext_w:ext_w + nodes] = hot_columns(column(base_mr + j), nodes)
         sel_mesh[:, at] = hot_rows(id_rows[base_mr + j:base_mr + j + 1, :], nodes)
     for o in range(3):
+        place = (0, 2, 1)[o]
         for b in range(blocks_d):
             j = o * blocks_d + b
-            at = slice(j * LANES, (j + 1) * LANES)
+            at = slice(place * width_d + b * LANES, place * width_d + (b + 1) * LANES)
             hot_dec[at, 0:nodes] = hot_columns(column(base_ds + j), nodes)
             hot_dec[at, nodes:nodes + cells] = hot_columns(column(base_dr + j), cells)
             live = lane + b * LANES < dec_counts[0, o]
             row = jnp.where(live, id_rows[base_dr + j:base_dr + j + 1, :], -1.0)
             sel_dec[:, at] = hot_rows(row, cells)
 
-    arrive(0)
-    for o in range(3):
-        joined = enc_table[o].astype(F32) + product(hot_columns(column(base_er + o), nodes), target)
-        hidden[o * width_e:(o + 1) * width_e, :] = silu(joined).astype(BF)
-    summed = product(jnp.concatenate(sel, axis=1), hidden[0:3 * width_e, :]).astype(BF)
-    summed = product(summed, weight("em")).astype(BF)
-    inner = silu(kept + product(summed, weight("ea"))).astype(BF)
-    mesh_state = mesh_state + norm_rows(product(inner, weight("ef")))
+    for h in range(2):
+        arrive(0, h)
+        for side in range(2):
+            joined = enc_table[h, side].astype(F32) + pre_enc[side, :, cols[h]]
+            hidden[h, side * width_e:(side + 1) * width_e, :] = silu(joined).astype(BF)
+        summed = summed_own[h] + product(sel_side, hidden[h, 0:2 * width_e, :])
+        acc = acc + product(summed.astype(BF), message_absorb[cols[h], :])
+    mesh_state = mesh_state + norm_rows(product(silu(acc).astype(BF), weight("ef")))
 
     chunk = 512
+    edges = blocks_m * LANES
     for l in range(layers):
         tag = str(l)
         mesh_low = mesh_state.astype(BF)
-        source = product(mesh_low, weight("ps" + tag)).astype(BF)
-        rim[l] = product(hot_halo, source).astype(BF)
-        exchange(1 + l, rim.at[l], rim.at[l], lows[1 + l], highs[1 + l])
-        tables[l, rim_w:rim_w + nodes, :] = source
-        tables[l, ext_w:ext_w + nodes, :] = product(mesh_low, weight("pt" + tag)).astype(BF)
-        kept = product(mesh_low, weight("pr" + tag))
+        w = weight("ps" + tag)
+        for h in range(2):
+            source = product(mesh_low, w[:, cols[h]]).astype(BF)
+            rim[l, h] = product(hot_halo, source).astype(BF)
+            exchange(1 + l, h, rim.at[l, h], rim.at[l, h])
+            own_table[h, 0:nodes, :] = source
+        w = weight("pt" + tag)
+        for h in range(2):
+            own_table[h, nodes:2 * nodes, :] = product(mesh_low, w[:, cols[h]]).astype(BF)
+        for h in range(2):
+            for c in range(edges // chunk):
+                at = slice(c * chunk, (c + 1) * chunk)
+                pre_mesh[h, at, :] = product(hot_mesh[at, 2 * rim_w:], own_table[h])
+        acc = product(mesh_low, weight("pr" + tag))
         if l == 0:
             grid_tgt[...] = product(latent, weight("dt")).astype(BF)
             grid_kept = product(latent, weight("dr"))
-        arrive(1 + l)
-        for c in range(blocks_m * LANES // chunk):
-            at = slice(c * chunk, (c + 1) * chunk)
-            hidden[at, :] = silu(product(hot_mesh[at, :], tables[l])).astype(BF)
-        summed = product(sel_mesh[...], hidden[...]).astype(BF)
-        inner = silu(kept + product(summed, weight("pa" + tag))).astype(BF)
-        mesh_state = mesh_state + norm_rows(product(inner, weight("pf" + tag)))
-
-    dec_table[1] = product(mesh_state.astype(BF), weight("ds")).astype(BF)
-    exchange(1 + layers, dec_table.at[1], dec_table.at[1], dec_table.at[0], dec_table.at[2])
-
-    def decode(o):
-        at = slice(o * width_d, (o + 1) * width_d)
-        joined = product(hot_dec[at, 0:nodes], dec_table[o]) + product(
-            hot_dec[at, nodes:nodes + cells], grid_tgt[...])
-        hidden[at, :] = silu(joined).astype(BF)
-
-    decode(1)
-    arrive(1 + layers)
-    decode(0)
-    decode(2)
-    summed = product(sel_dec[...], hidden[0:3 * width_d, :]).astype(BF)
-    summed = product(summed, weight("dm")).astype(BF)
-    inner = silu(grid_kept + product(summed, weight("da"))).astype(BF)
-    out[...] = product_nt(readout_t[...], inner).astype(BF)
-
-    for one, two in sent:
+        if l == layers - 1:
+            for h in range(2):
+                pre_dec[h] = product(hot_dec[:, nodes:], grid_tgt[:, cols[h]])
+            message_absorb = join_weights("dm", "da")
+        w = weight("pa" + tag)
+        for h in range(2):
+            arrive(1 + l, h)
+            for c in range(edges // chunk):
+                at = slice(c * chunk, (c + 1) * chunk)
+                joined = pre_mesh[h, at, :] + product(hot_mesh[at, 0:2 * rim_w], rim_table[l, h])
+                hidden[h, at, :] = silu(joined).astype(BF)
+            summed = product(sel_mesh[...], hidden[h]).astype(BF)
+            acc = acc + product(summed, w[cols[h], :])
+        mesh_state = mesh_state + norm_rows(product(silu(acc).astype(BF), weight("pf" + tag)))
+
+    mesh_low = mesh_state.astype(BF)
+    w = weight("ds")
+    for h in range(2):
+        own_table[h, 0:nodes, :] = product(mesh_low, w[:, cols[h]]).astype(BF)
+        exchange(1 + layers, h, own_table.at[h, pl.ds(0, nodes)], own_table.at[h, pl.ds(0, nodes)])
+
+    def decode(h, place, table):
+        at = slice(place * width_d, (place + 1) * width_d)
+        joined = pre_dec[h, at, :] + product(hot_dec[at, 0:nodes], table)
+        hidden[h, at, :] = silu(joined).astype(BF)
+
+    summed_own = []
+    for h in range(2):
+        decode(h, 2, own_table[h, 0:nodes, :])
+        summed_own.append(product(sel_dec[:, 2 * width_d:], hidden[h, 2 * width_d:3 * width_d, :]))
+    acc = grid_kept
+    for h in range(2):
+        arrive(1 + layers, h)
+        decode(h, 0, dec_table[h, 0])
+        decode(h, 1, dec_table[h, 1])
+        summed = summed_own[h] + product(sel_dec[:, 0:2 * width_d], hidden[h, 0:2 * width_d, :])
+        acc = acc + product(summed.astype(BF), message_absorb[cols[h], :])
+    out[...] = product_nt(readout_t[...], silu(acc).astype(BF)).astype(BF)
+
+    for one, two in sent.values():
         @pl.when(has_left)
         def _(one=one):
             one.wait_send()
@@ -357,6 +405,7 @@
     width_d = backward_icosa_emitters.size // 3
     n_weights = 11 + 5 * layers
     rounds = 2 + layers
+    half = dim // 2
     vmem = pl.BlockSpec(memory_space=pltpu.VMEM)
     smem = pl.BlockSpec(memory_space=pltpu.SMEM)
     far = pl.BlockSpec(memory_space=pl.ANY)
@@ -369,20 +418,24 @@
             pltpu.VMEM((n_weights, dim, dim), BF),
             pltpu.VMEM((LANES, LANES), F32),
             pltpu.VMEM((LANES, LANES), F32),
-            pltpu.VMEM((2, width_e, dim), BF),
-            pltpu.VMEM((3, width_e, dim), BF),
-            pltpu.VMEM((layers, rim_w, dim), BF),
-            pltpu.VMEM((layers, 2 * rim_w + 2 * nodes, dim), BF),
-            pltpu.VMEM((3, nodes, dim), BF),
+            pltpu.VMEM((2, 2, width_e, half), BF),
+            pltpu.VMEM((2, 2, width_e, half), BF),
+            pltpu.VMEM((2, width_e, dim), F32),
+            pltpu.VMEM((layers, 2, rim_w, half), BF),
+            pltpu.VMEM((layers, 2, 2 * rim_w, half), BF),
+            pltpu.VMEM((2, 2 * nodes, half), BF),
+            pltpu.VMEM((2, edges, half), F32),
+            pltpu.VMEM((2, 2, nodes, half), BF),
+            pltpu.VMEM((2, 3 * width_d, half), F32),
             pltpu.VMEM((cells, dim), BF),
             pltpu.VMEM((edges, 2 * rim_w + 2 * nodes), BF),
             pltpu.VMEM((nodes, edges), BF),
             pltpu.VMEM((3 * width_d, nodes + cells), BF),
             pltpu.VMEM((cells, 3 * width_d), BF),
-            pltpu.VMEM((edges, dim), BF),
+            pltpu.VMEM((2, edges, half), BF),
             pltpu.SemaphoreType.DMA((n_weights,)),
-            pltpu.SemaphoreType.DMA((2 * rounds,)),
-            pltpu.SemaphoreType.DMA((2 * rounds,)),
+            pltpu.SemaphoreType.DMA((4 * rounds,)),
+            pltpu.SemaphoreType.DMA((4 * rounds,)),
         ],
         compiler_params=pltpu.CompilerParams(
             collective_id=0, has_side_effects=True, vmem_limit_bytes=56 * 1024 * 1024

time: 37.9 us -> 34.9 us (0.921)
  Pallas kernels: 36.1 us -> 33.2 us
    pallas_call x1, Pallas kernels: 36.1 us -> 33.2 us  [body(): pl.pallas_call(functools.partial(kernel, n), out_shape=jax.ShapeDtypeStru...]
where the time goes in v2:
time: 34.9 us; the launch traced here: 34.7 us
  Pallas kernels  33.2 us (95%)
  local copies, waits for them, and re-layouts  1.56 us (4%)
    pallas_call x1, Pallas kernels, body(): pl.pallas_call(functools.partial(kernel, n), out_shape=jax.ShapeDtypeStru...  33.2 us
    unnamed x1, local copies, waits for them, and re-layouts  1.56 us

profile of v2, /device:TPU:14, one launch (start us, length us, event | category | flops | bytes accessed | tf_op | source)
XLA Modules:
  0.0 34.7 jit_solution(1709172996989126002)
XLA Ops:
  0.0 33.2 %shard_map.280 = bf16[227,256]{1,0:T(8,128)(2,1)} custom-call(bf16[474,256]{1,0:T(8,128)(2,1)} %bitcast.4, f32[3,256]{1,0:T(4,128)} %static.1, s32[1,3,1,128]{3,2,1,0:T(1,128)} %enc_send.1, s32[1,3,1,128]{3,2,1,0:T(1,128)} %enc_recv.1, s32[1,3]{1,0:T(1,128)} %enc_counts.1, s32[16,128]{1,0:T(8,128)} %mesh_send.1, s32[16,128]{1,0:T(8,128)} %mesh_recv.1, ...), custom_call_target="tpu_custom_call" | custom-call | tf_op jit(solution)/shard_map/pallas_call | solution.py:412
  33.2 1.6 %copy.32 = bf16[256,227]{0,1:T(8,128)(2,1)} copy(bf16[256,227]{0,1:T(8,128)(2,1)} %bitcast.3) | data formatting | bytes 232448

commit v3 on v2

--- a/solution.py
+++ b/solution.py
@@ -160,7 +160,10 @@
         for l in range(layers):
             lows[1 + l, h] = rim_table.at[l, h, pl.ds(0, rim_w)]
             highs[1 + l, h] = rim_table.at[l, h, pl.ds(rim_w, rim_w)]
-        lows[1 + layers, h], highs[1 + layers, h] = dec_table.at[h, 0], dec_table.at[h, 1]
+        for g in range(2):
+            part = pl.ds(g * (nodes // 2), nodes // 2)
+            lows[1 + layers + g, h] = dec_table.at[h, 0, part]
+            highs[1 + layers + g, h] = dec_table.at[h, 1, part]
 
     sent = {}
 
@@ -326,13 +329,20 @@
                 hidden[h, at, :] = silu(joined).astype(BF)
             summed = product(sel_mesh[...], hidden[h]).astype(BF)
             acc = acc + product(summed, w[cols[h], :])
-        mesh_state = mesh_state + norm_rows(product(silu(acc).astype(BF), weight("pf" + tag)))
-
-    mesh_low = mesh_state.astype(BF)
+        if l < layers - 1:
+            mesh_state = mesh_state + norm_rows(product(silu(acc).astype(BF), weight("pf" + tag)))
+
+    w_finish = weight("pf" + str(layers - 1))
     w = weight("ds")
-    for h in range(2):
-        own_table[h, 0:nodes, :] = product(mesh_low, w[:, cols[h]]).astype(BF)
-        exchange(1 + layers, h, own_table.at[h, pl.ds(0, nodes)], own_table.at[h, pl.ds(0, nodes)])
+    for g in range(2):
+        first = g * (nodes // 2)
+        at = slice(first, first + nodes // 2)
+        inner = silu(acc[at]).astype(BF)
+        mesh_low = (mesh_state[at] + norm_rows(product(inner, w_finish))).astype(BF)
+        for h in range(2):
+            own_table[h, at, :] = product(mesh_low, w[:, cols[h]]).astype(BF)
+            part = own_table.at[h, pl.ds(first, nodes // 2)]
+            exchange(1 + layers + g, h, part, part)
 
     def decode(h, place, table):
         at = slice(place * width_d, (place + 1) * width_d)
@@ -346,6 +356,7 @@
     acc = grid_kept
     for h in range(2):
         arrive(1 + layers, h)
+        arrive(2 + layers, h)
         decode(h, 0, dec_table[h, 0])
         decode(h, 1, dec_table[h, 1])
         summed = summed_own[h] + product(sel_dec[:, 0:2 * width_d], hidden[h, 0:2 * width_d, :])
@@ -404,7 +415,7 @@
     width_e = encoder_senders.size // 3
     width_d = backward_icosa_emitters.size // 3
     n_weights = 11 + 5 * layers
-    rounds = 2 + layers
+    rounds = 3 + layers
     half = dim // 2
     vmem = pl.BlockSpec(memory_space=pltpu.VMEM)
     smem = pl.BlockSpec(memory_space=pltpu.SMEM)

time: 34.9 us -> 34.9 us (level)
  no operation moved by 1% of the time
where the time goes in v3:
time: 34.9 us; the launch traced here: 34.8 us
  Pallas kernels  33.2 us (95%)
  local copies, waits for them, and re-layouts  1.56 us (4%)
    pallas_call x1, Pallas kernels, body(): pl.pallas_call(functools.partial(kernel, n), out_shape=jax.ShapeDtypeStru...  33.2 us
    unnamed x1, local copies, waits for them, and re-layouts  1.56 us

profile of v3, /device:TPU:14, one launch (start us, length us, event | category | flops | bytes accessed | tf_op | source)
XLA Modules:
  0.0 34.8 jit_solution(6188523480372168958)
XLA Ops:
  0.0 33.2 %shard_map.280 = bf16[227,256]{1,0:T(8,128)(2,1)} custom-call(bf16[474,256]{1,0:T(8,128)(2,1)} %bitcast.4, f32[3,256]{1,0:T(4,128)} %static.1, s32[1,3,1,128]{3,2,1,0:T(1,128)} %enc_send.1, s32[1,3,1,128]{3,2,1,0:T(1,128)} %enc_recv.1, s32[1,3]{1,0:T(1,128)} %enc_counts.1, s32[16,128]{1,0:T(8,128)} %mesh_send.1, s32[16,128]{1,0:T(8,128)} %mesh_recv.1, ...), custom_call_target="tpu_custom_call" | custom-call | tf_op jit(solution)/shard_map/pallas_call | solution.py:423
  33.2 1.6 %copy.32 = bf16[256,227]{0,1:T(8,128)(2,1)} copy(bf16[256,227]{0,1:T(8,128)(2,1)} %bitcast.3) | data formatting | bytes 232448
